TPU v7x, 32 devices: a whole 2x2x4 slice. The times are simulated.
32 devices in a mesh: dp: 4 (over x, core), blk: 8 (over z, y).
Axes of the slice: x: 2, y: 2, z: 4, core: 2. Of those that a mesh axis runs over, the one named last changes fastest.
Arguments:
- query: bfloat16 [256, 768], P(('dp', 'blk')), parts along dimension 0, may hold values from -6 to 6
- keys: bfloat16 [8192, 768], P(('dp', 'blk')), parts along dimension 0, may hold values from -6 to 6
- values: bfloat16 [8192, 768], P(('dp', 'blk')), parts along dimension 0, may hold values from -6 to 6
- attn_out: bfloat16 [256, 768], P(('dp', 'blk')), parts along dimension 0, may hold values from -1.5 to 1.5
- out_grad: bfloat16 [256, 768], P(('dp', 'blk')), parts along dimension 0, may hold values from -3072 to 3072
- lse: float32 [6, 256], P(None, ('dp', 'blk')), parts along dimension 1, may hold values from 8.5 to 11
- lengths: int32 [256], P(('dp', 'blk')), parts along dimension 0, may hold values from 256 to 2048
Outputs:
- query_grad: bfloat16 [256, 768], P(('dp', 'blk')), parts along dimension 0
- key_grad: bfloat16 [8192, 768], P(('dp', 'blk')), parts along dimension 0
- value_grad: bfloat16 [8192, 768], P(('dp', 'blk')), parts along dimension 0
There are 4 independent parts, one for each index of `dp`. A program takes and returns all parts, laid end to end along the dimension named above; each array names one. Nothing has to cross between parts.
All inputs are finite; a program needn't handle non-finite values.
Results may differ from a plain program's by a relative error of at most 0.005.
Values may be sent and summed in bfloat16 or wider, within the bound.
A program may use at most 64 MiB of HBM per device.

v0:
```python
import math

import jax
import jax.numpy as jnp
from jax import lax
from jax.sharding import PartitionSpec as P


def row_delta(grads, outputs, head_count):
    product = grads.astype(jnp.float32) * outputs.astype(jnp.float32)
    return product.reshape(grads.shape[0], head_count, -1).sum(axis=-1).T


def local(query, keys, values, attn_out, out_grad, lse, lengths):
    head_count = lse.shape[0]
    key_rows = keys.shape[0]
    head_width = keys.shape[1] // head_count
    scale = 1.0 / math.sqrt(head_width)
    query_all, grad_all, output_all = (
        lax.all_gather(query, "blk", axis=0, tiled=True),
        lax.all_gather(out_grad, "blk", axis=0, tiled=True),
        lax.all_gather(attn_out, "blk", axis=0, tiled=True),
    )
    lse_all = lax.all_gather(lse, "blk", axis=1, tiled=True)
    delta_all = row_delta(grad_all, output_all, head_count)
    lengths_all = lax.all_gather(lengths, "blk", axis=0, tiled=True)
    positions = lax.axis_index("blk") * key_rows + jnp.arange(key_rows, dtype=jnp.int32)
    visible = positions[None, :] < lengths_all[:, None]
    key_parts, value_parts, score_grads = ([], [], [])
    for head in range(head_count):
        low = head * head_width
        query_h = query_all[:, low : low + head_width]
        keys_h = keys[:, low : low + head_width]
        values_h = values[:, low : low + head_width]
        grad_h = grad_all[:, low : low + head_width]
        scores = jnp.dot(query_h, keys_h.T, preferred_element_type=jnp.float32) * scale
        probs = jnp.where(visible, jnp.exp(scores - lse_all[head][:, None]), jnp.float32(0.0))
        probs_low = probs.astype(jnp.bfloat16)
        value_parts.append(jnp.dot(probs_low.T, grad_h, preferred_element_type=jnp.float32))
        prob_grad = jnp.dot(grad_h, values_h.T, preferred_element_type=jnp.float32)
        score_grad = (probs * (prob_grad - delta_all[head][:, None]) * scale).astype(jnp.bfloat16)
        key_parts.append(jnp.dot(score_grad.T, query_h, preferred_element_type=jnp.float32))
        score_grads.append(score_grad)
    pieces = []
    for head in range(head_count):
        low = head * head_width
        rows_h = score_grads[head]
        pieces.append(
            jnp.dot(rows_h, keys[:, low : low + head_width], preferred_element_type=jnp.float32)
        )
    terms = jnp.concatenate(pieces, axis=1)
    summed = lax.psum_scatter(terms, "blk", scatter_dimension=0, tiled=True)
    query_grad = summed.astype(jnp.bfloat16)
    key_grad = jnp.concatenate(key_parts, axis=1).astype(jnp.bfloat16)
    value_grad = jnp.concatenate(value_parts, axis=1).astype(jnp.bfloat16)
    return (query_grad, key_grad, value_grad)


def solution(mesh):
    in_specs = (
        P(("dp", "blk"), None),
        P(("dp", "blk"), None),
        P(("dp", "blk"), None),
        P(("dp", "blk"), None),
        P(("dp", "blk"), None),
        P(None, ("dp", "blk")),
        P(("dp", "blk")),
    )
    out_specs = (P(("dp", "blk"), None), P(("dp", "blk"), None), P(("dp", "blk"), None))
    return jax.shard_map(local, mesh=mesh, in_specs=in_specs, out_specs=out_specs, check_vma=False)
```

profile of v0, /device:TPU:0, one launch (start us, length us, event | category | flops | bytes accessed | tf_op | source)
XLA Modules:
  0.0 219.1 jit_solution(7707254223375097057)
XLA Ops:
  7.2 0.6 copy-done.4
  7.8 0.6 dynamic-slice
  9.1 0.9 dynamic-update-slice
  9.9 13.1 %all-reduce = s32[64]{0:T(128)S(1)} all-reduce(s32[64]{0:T(128)S(1)} %dynamic-update-slice), channel_id=1, replica_groups=mesh['dp'=4,'blk'=8] {'blk'}, use_global_device_ids=true, to_apply=%add | all-reduce | flops 64 | bytes 512
  23.0 0.8 copy.17
  23.7 30.4 %all_gather.17 = f32[6,64]{0,1:T(8,128)S(1)} all-gather(f32[6,8]{0,1:T(8,128)S(1)} %copy.17), channel_id=1, replica_groups=mesh['dp'=4,'blk'=8] {'blk'}, dimensions={1}, use_global_device_ids=true | all-gather | bytes 1728 | tf_op jit(solution)/shard_map/all_gather | solution.py:24
  54.1 0.3 slice_reduce_fusion.1
  54.4 30.8 %all_gather.18 = bf16[64,768]{1,0:T(8,128)(2,1)S(1)} all-gather(bf16[8,768]{1,0:T(8,128)(2,1)} %param.11), channel_id=1, replica_groups=mesh['dp'=4,'blk'=8] {'blk'}, dimensions={0}, use_global_device_ids=true | all-gather | bytes 110592 | tf_op jit(solution)/shard_map/all_gather | solution.py:21
  85.2 30.7 %all_gather.16 = bf16[64,768]{1,0:T(8,128)(2,1)S(1)} all-gather(bf16[8,768]{1,0:T(8,128)(2,1)} %param.7), channel_id=1, replica_groups=mesh['dp'=4,'blk'=8] {'blk'}, dimensions={0}, use_global_device_ids=true | all-gather | bytes 110592 | tf_op jit(solution)/shard_map/all_gather | solution.py:20
  117.0 0.5 copy-done.3
  117.5 30.5 %all_gather.19 = bf16[64,768]{1,0:T(8,128)(2,1)S(1)} all-gather(bf16[8,768]{1,0:T(8,128)(2,1)S(1)} %copy-done.3), channel_id=1, replica_groups=mesh['dp'=4,'blk'=8] {'blk'}, dimensions={0}, use_global_device_ids=true | all-gather | bytes 110592 | tf_op jit(solution)/shard_map/all_gather | solution.py:22
  148.3 0.3 slice_reduce_fusion
  148.5 0.5 copy-done.1
  150.9 0.7 copy-done.2
  151.8 0.2 fusion.11
  152.0 0.2 fusion.4
  152.4 0.2 fusion.2
  152.7 0.2 fusion.1
  153.1 0.9 copy.19
  154.2 0.2 fusion.9
  154.5 0.2 fusion.8
  155.1 0.9 copy.18
  156.0 54.9 %reduce-scatter.2.cloned.1.call-done = f32[8,768]{1,0:T(8,128)} async-done(((f32[64,768]{1,0:T(8,128)}), f32[8,768]{1,0:T(8,128)}) %reduce-scatter.2.cloned.1.call-update) | async-done | bytes 24592 | tf_op jit(solution)/shard_map/reduce_scatter | solution.py:52
  210.9 1.3 convert_element_type.55
  (37 shorter events, 4.3 us)
Async XLA Ops:
  7.2 0.7 copy-start.4
  7.2 108.8 %copy-start = (bf16[256,768]{1,0:T(8,128)(2,1)S(1)}, bf16[256,768]{1,0:T(8,128)(2,1)}, u32[]{:S(2)}) copy-start(bf16[256,768]{1,0:T(8,128)(2,1)} %param.8) | copy-start | bytes 1179652
  7.2 203.7 %reduce-scatter.2.cloned.1.call-start = ((), (), s32[]{:S(2)}) async-start(), calls=%async_computation.1 | async-start | bytes 221184 | tf_op jit(solution)/shard_map/reduce_scatter | solution.py:52
  116.8 0.7 copy-start.3
  148.1 1.0 copy-start.1
  150.9 0.7 copy-start.2
Sparse Core Ops, SparseCore 0:
  151.7 59.1 reduce-scatter.1
where the time goes:
time: 219 us
  blocking collectives  136 us (62%)
  waiting for transfers between devices  54.9 us (25%)
  between operations  14.9 us (7%)
  local copies, waits for them, and re-layouts  6.95 us (3%)
  matrix products  5.26 us (2%)
    reduce_scatter x1, waiting for transfers between devices, local(): summed = lax.psum_scatter(terms, 'blk', scatter_dimension=0, tiled=True)  54.9 us
    all_gather x1, blocking collectives, local(): lax.all_gather(out_grad, 'blk', axis=0, tiled=True)  30.8 us
    all_gather x1, blocking collectives, local(): lax.all_gather(query, 'blk', axis=0, tiled=True)  30.7 us
    all_gather x1, blocking collectives, local(): lax.all_gather(attn_out, 'blk', axis=0, tiled=True)  30.5 us
    all_gather x1, blocking collectives, local(): lse_all = lax.all_gather(lse, 'blk', axis=1, tiled=True)  30.4 us
    unnamed x1, blocking collectives  13.1 us
    unnamed x16, local copies, waits for them, and re-layouts  6.37 us
  transfers between devices with their start and end apart: 1, of which 1 were waited for; matrix products, arithmetic and copies ran while one was open for 2% of the time, Pallas kernels for 0%

commit v1 on v0

v1 whole, which is shorter than its diff:
```python
import functools
import math

import jax
import jax.numpy as jnp
from jax import lax
from jax.experimental import pallas as pl
from jax.experimental.pallas import tpu as pltpu
from jax.sharding import PartitionSpec as P

HEADS_PER_GROUP = 2
CHUNK_SLOTS = 8
UNROLL_LIMIT = 16
F32 = jnp.float32
BF16 = jnp.bfloat16


def over(count, body):
    if count <= UNROLL_LIMIT:
        for i in range(count):
            body(i)
    else:
        lax.fori_loop(0, count, lambda i, c: (body(i), c)[1], 0)


def kernel(
    n, heads, width,
    query, keys, values, attn_out, out_grad, lse, lengths,
    dq_out, dk_out, dv_out,
    q_own, o_own, g_own, lse_own, len_own, k_in, v_in,
    msg, aux, msg_recv, aux_recv, q_all, g_all, p_all, s_all,
    part, part_recv, own_part, dq, dk, dv,
    in_sem, out_sem, aux_send, aux_sem, msg_send, msg_sem, part_send, part_sem,
):
    me = lax.axis_index("blk")
    rows = q_own.shape[0]
    key_rows = k_in.shape[0]
    group_width = HEADS_PER_GROUP * width
    groups = heads // HEADS_PER_GROUP
    scale = 1.0 / math.sqrt(width)
    chunk_slots = min(n, CHUNK_SLOTS)
    chunk_rows = chunk_slots * rows

    small = [(query, q_own), (attn_out, o_own), (out_grad, g_own), (lse, lse_own), (lengths, len_own)]
    large = [(keys, k_in), (values, v_in)]
    copies = [pltpu.make_async_copy(a, b, in_sem.at[i]) for i, (a, b) in enumerate(small + large)]
    for copy in copies:
        copy.start()

    barrier = pltpu.get_barrier_semaphore()

    def greet(i):
        pl.semaphore_signal(
            barrier, inc=1, device_id={"blk": lax.rem(me + i + 1, n)}, device_id_type=pl.DeviceIdType.MESH
        )

    over(n - 1, greet)

    for copy in copies[: len(small)]:
        copy.wait()
    q32, g32 = q_own[...].astype(F32), g_own[...].astype(F32)
    own = jnp.concatenate([q32, g32], axis=0).astype(BF16)
    for g in range(groups):
        piece = own[:, g * group_width : (g + 1) * group_width]
        msg[g] = piece
        msg_recv[g, n - 1] = piece
    product = g32 * o_own[...].astype(F32)
    lane = lax.broadcasted_iota(jnp.int32, (rows, 128), 1)
    eye = lax.broadcasted_iota(jnp.int32, (rows, rows), 0) == lax.broadcasted_iota(jnp.int32, (rows, rows), 1)

    def column(row):
        return jnp.sum(jnp.where(eye, jnp.broadcast_to(row, (rows, rows)), 0.0), axis=1, keepdims=True)

    table = jnp.where(lane == 2 * heads, column(len_own[...].astype(F32)), 0.0)
    for h in range(heads):
        delta = jnp.sum(product[:, h * width : (h + 1) * width], axis=1, keepdims=True)
        table = jnp.where(lane == h, column(lse_own[h : h + 1, :]), table)
        table = jnp.where(lane == heads + h, delta, table)
    aux[...] = table
    aux_recv[n - 1] = table

    pl.semaphore_wait(barrier, n - 1)

    def remote(src, dst, send, recv, peer):
        return pltpu.make_async_remote_copy(
            src_ref=src, dst_ref=dst, send_sem=send, recv_sem=recv,
            device_id={"blk": peer}, device_id_type=pl.DeviceIdType.MESH,
        )

    def send_aux(i):
        remote(aux, aux_recv.at[i], aux_send, aux_sem, lax.rem(me + i + 1, n)).start()

    over(n - 1, send_aux)
    for g in range(groups):

        def send_msg(i, g=g):
            remote(
                msg.at[g], msg_recv.at[g, i], msg_send.at[g], msg_sem.at[g], lax.rem(me + i + 1, n)
            ).start()

        over(n - 1, send_msg)

    def all_of(ref, sem):
        whole = ref.at[pl.ds(0, n - 1)]
        pltpu.make_async_copy(whole, whole, sem).wait()

    for copy in copies[len(small) :]:
        copy.wait()
    all_of(aux_recv, aux_sem)

    position = me * key_rows + lax.broadcasted_iota(jnp.int32, (chunk_rows, key_rows), 1)
    position = position.astype(F32)

    for g in range(groups):
        all_of(msg_recv.at[g], msg_sem.at[g])

        def attend(c, g=g):
            slots = pl.ds(c * chunk_slots, chunk_slots)
            lines = pl.ds(c * chunk_rows, chunk_rows)
            got = msg_recv[g, slots].astype(F32)
            q_c = got[:, :rows].reshape(chunk_rows, group_width).astype(BF16)
            g_c = got[:, rows:].reshape(chunk_rows, group_width).astype(BF16)
            q_all[g, lines] = q_c
            g_all[g, lines] = g_c
            facts = aux_recv[slots].reshape(chunk_rows, 128)
            visible = position < facts[:, 2 * heads : 2 * heads + 1]
            parts = []
            for j in range(HEADS_PER_GROUP):
                h = g * HEADS_PER_GROUP + j
                cols = slice(h * width, (h + 1) * width)
                mine = slice(j * width, (j + 1) * width)
                k_h, v_h = k_in[:, cols], v_in[:, cols]
                nt = (((1,), (1,)), ((), ()))
                scores = lax.dot_general(q_c[:, mine], k_h, nt, preferred_element_type=F32) * scale
                probs = jnp.where(visible, jnp.exp(scores - facts[:, h : h + 1]), 0.0)
                prob_grad = lax.dot_general(g_c[:, mine], v_h, nt, preferred_element_type=F32)
                delta = facts[:, heads + h : heads + h + 1]
                score_grad = (probs * (prob_grad - delta) * scale).astype(BF16)
                p_all[h, lines] = probs.astype(BF16)
                s_all[h, lines] = score_grad
                term = jnp.dot(score_grad, k_h, preferred_element_type=F32)
                parts.append(term.reshape(chunk_slots, rows, width))
            terms = jnp.concatenate(parts, axis=1)
            part[g, slots] = terms.astype(BF16)
            return terms

        if n == chunk_slots:
            own_part[g] = attend(0)[n - 1]
        else:

            def step(c, carry):
                own_part[g] = attend(c)[chunk_slots - 1]
                return carry

            lax.fori_loop(0, n // chunk_slots, step, 0)

        def send_part(i, g=g):
            remote(
                part.at[g, i], part_recv.at[g, i], part_send.at[g], part_sem.at[g], lax.rem(me + n - i - 1, n)
            ).start()

        over(n - 1, send_part)

    tn = (((0,), (0,)), ((), ()))
    results = []
    for g in range(groups):
        for j in range(HEADS_PER_GROUP):
            h = g * HEADS_PER_GROUP + j
            cols = slice(h * width, (h + 1) * width)
            mine = slice(j * width, (j + 1) * width)
            dv[:, cols] = lax.dot_general(p_all[h], g_all[g, :, mine], tn, preferred_element_type=F32).astype(BF16)
            dk[:, cols] = lax.dot_general(s_all[h], q_all[g, :, mine], tn, preferred_element_type=F32).astype(BF16)
    for i, (a, b) in enumerate([(dk, dk_out), (dv, dv_out)]):
        copy = pltpu.make_async_copy(a, b, out_sem.at[i])
        copy.start()
        results.append(copy)

    for g in range(groups):
        all_of(part_recv.at[g], part_sem.at[g])

        def add(i, total, g=g):
            return total + part_recv[g, i].astype(F32)

        total = own_part[g]
        if n <= UNROLL_LIMIT:
            for i in range(n - 1):
                total = add(i, total)
        else:
            total = lax.fori_loop(0, n - 1, add, total)
        for j in range(HEADS_PER_GROUP):
            h = g * HEADS_PER_GROUP + j
            dq[:, h * width : (h + 1) * width] = total[j * rows : (j + 1) * rows].astype(BF16)
    copy = pltpu.make_async_copy(dq, dq_out, out_sem.at[2])
    copy.start()
    results.append(copy)

    all_of(aux_recv, aux_send)
    for g in range(groups):
        all_of(msg_recv.at[g], msg_send.at[g])
        all_of(part_recv.at[g], part_send.at[g])
    for copy in results:
        copy.wait()


def local(n, query, keys, values, attn_out, out_grad, lse, lengths):
    heads, rows = lse.shape
    key_rows, columns = keys.shape
    width = columns // heads
    groups = heads // HEADS_PER_GROUP
    group_width = HEADS_PER_GROUP * width
    total = n * rows
    anywhere = pl.BlockSpec(memory_space=pltpu.HBM)
    vmem = pltpu.VMEM
    dma = pltpu.SemaphoreType.DMA
    return pl.pallas_call(
        functools.partial(kernel, n, heads, width),
        out_shape=(
            jax.ShapeDtypeStruct(query.shape, BF16),
            jax.ShapeDtypeStruct(keys.shape, BF16),
            jax.ShapeDtypeStruct(values.shape, BF16),
        ),
        in_specs=[anywhere] * 7,
        out_specs=(anywhere,) * 3,
        scratch_shapes=[
            vmem(query.shape, BF16),
            vmem(query.shape, BF16),
            vmem(query.shape, BF16),
            vmem(lse.shape, F32),
            vmem((1, rows), jnp.int32),
            vmem(keys.shape, BF16),
            vmem(values.shape, BF16),
            vmem((groups, 2 * rows, group_width), BF16),
            vmem((rows, 128), F32),
            vmem((groups, n, 2 * rows, group_width), BF16),
            vmem((n, rows, 128), F32),
            vmem((groups, total, group_width), BF16),
            vmem((groups, total, group_width), BF16),
            vmem((heads, total, key_rows), BF16),
            vmem((heads, total, key_rows), BF16),
            vmem((groups, n, HEADS_PER_GROUP * rows, width), BF16),
            vmem((groups, n, HEADS_PER_GROUP * rows, width), BF16),
            vmem((groups, HEADS_PER_GROUP * rows, width), F32),
            vmem(query.shape, BF16),
            vmem(keys.shape, BF16),
            vmem(values.shape, BF16),
            dma((7,)),
            dma((3,)),
            dma(()),
            dma(()),
            dma((groups,)),
            dma((groups,)),
            dma((groups,)),
            dma((groups,)),
        ],
        compiler_params=pltpu.CompilerParams(
            collective_id=0, has_side_effects=True, vmem_limit_bytes=40 * 1024 * 1024
        ),
        name="cross_attention_backward",
    )(query, keys, values, attn_out, out_grad, lse, lengths.reshape(1, rows))


def solution(mesh):
    in_specs = (
        P(("dp", "blk"), None),
        P(("dp", "blk"), None),
        P(("dp", "blk"), None),
        P(("dp", "blk"), None),
        P(("dp", "blk"), None),
        P(None, ("dp", "blk")),
        P(("dp", "blk")),
    )
    out_specs = (P(("dp", "blk"), None), P(("dp", "blk"), None), P(("dp", "blk"), None))
    body = functools.partial(local, mesh.shape["blk"])
    return jax.shard_map(body, mesh=mesh, in_specs=in_specs, out_specs=out_specs, check_vma=False)
```

time: 219 us -> 27 us (0.12)
  blocking collectives: 136 us -> 0 us
  waiting for transfers between devices: 54.9 us -> 0 us
  Pallas kernels: 0 us -> 18.4 us
  between operations: 14.9 us -> 0.66 us
  matrix products: 5.26 us -> 0 us
    all_gather x4 -> x0, blocking collectives: 122 us -> none  [the longest x1 30.8 us: local(): lax.all_gather(out_grad, 'blk', axis=0, tiled=True)]
    reduce_scatter x1 -> x0, waiting for transfers between devices: 54.9 us -> none  [local(): summed = lax.psum_scatter(terms, 'blk', scatter_dimension=0, tiled=True)]
    pallas_call x0 -> x1, Pallas kernels: none -> 18.4 us  [local(): pl.pallas_call(functools.partial(kernel, n, heads, width), out_shape=(jax...]
    unnamed x1 -> x0, blocking collectives: 13.1 us -> none
    dot_general x30 -> x0, matrix products: 5.26 us -> none  [the longest x6 1.26 us: local(): jnp.dot(probs_low.T, grad_h, preferred_element_type=jnp.float32)]
    unnamed x16 -> x17, local copies, waits for them, and re-layouts: 6.37 us -> 7.54 us
  transfers between devices with their start and end apart: 1 -> 0, of which waited for: 1 -> 0; matrix products, arithmetic and copies ran while one was open for 2% -> 0% of each run, Pallas kernels for 0% -> 0%
where the time goes in v1:
time: 27 us; the launch traced here: 26.6 us
  Pallas kernels  18.4 us (68%)
  local copies, waits for them, and re-layouts  7.54 us (28%)
  between operations  0.66 us (2%)
    pallas_call x1, Pallas kernels, local(): pl.pallas_call(functools.partial(kernel, n, heads, width), out_shape=(jax...  18.4 us
    unnamed x17, local copies, waits for them, and re-layouts  7.54 us

profile of v1, /device:TPU:0, one launch (start us, length us, event | category | flops | bytes accessed | tf_op | source)
XLA Modules:
  0.0 26.6 jit_solution(17335741564300640996)
XLA Ops:
  0.6 0.0 copy-start.6
  0.6 0.6 %copy-done.6 = s32[8]{0:T(128)S(1)} copy-done((s32[8]{0:T(128)S(1)}, s32[8]{0:T(128)}, u32[]{:S(2)}) %copy-start.6) | copy-done | bytes 56
  1.3 0.0 copy-start
  1.3 1.0 %copy-done = bf16[256,768]{1,0:T(8,128)(2,1)S(1)} copy-done((bf16[256,768]{1,0:T(8,128)(2,1)S(1)}, bf16[256,768]{1,0:T(8,128)(2,1)}, u32[]{:S(2)}) %copy-start) | copy-done | bytes 393240
  2.3 0.0 copy-start.1
  2.3 1.0 %copy-done.1 = bf16[256,768]{1,0:T(8,128)(2,1)S(1)} copy-done((bf16[256,768]{1,0:T(8,128)(2,1)S(1)}, bf16[256,768]{1,0:T(8,128)(2,1)}, u32[]{:S(2)}) %copy-start.1) | copy-done | bytes 393240
  3.3 0.0 copy-start.2
  3.3 0.7 %copy-done.2 = bf16[8,768]{1,0:T(8,128)(2,1)S(1)} copy-done((bf16[8,768]{1,0:T(8,128)(2,1)S(1)}, bf16[8,768]{1,0:T(8,128)(2,1)}, u32[]{:S(2)}) %copy-start.2) | copy-done | bytes 12312
  4.0 0.0 copy-start.3
  4.0 0.7 %copy-done.3 = bf16[8,768]{1,0:T(8,128)(2,1)S(1)} copy-done((bf16[8,768]{1,0:T(8,128)(2,1)S(1)}, bf16[8,768]{1,0:T(8,128)(2,1)}, u32[]{:S(2)}) %copy-start.3) | copy-done | bytes 12312
  4.7 0.0 copy-start.4
  4.7 0.7 %copy-done.4 = bf16[8,768]{1,0:T(8,128)(2,1)S(1)} copy-done((bf16[8,768]{1,0:T(8,128)(2,1)S(1)}, bf16[8,768]{1,0:T(8,128)(2,1)}, u32[]{:S(2)}) %copy-start.4) | copy-done | bytes 12312
  5.4 0.0 copy-start.5
  5.4 0.7 %copy-done.5 = f32[6,8]{1,0:T(8,128)S(1)} copy-done((f32[6,8]{1,0:T(8,128)S(1)}, f32[6,8]{1,0:T(8,128)}, u32[]{:S(2)}) %copy-start.5) | copy-done | bytes 216
  6.1 18.4 %cross_attention_backward.1 = (bf16[8,768]{1,0:T(8,128)(2,1)S(1)}, bf16[256,768]{1,0:T(8,128)(2,1)S(1)}, bf16[256,768]{1,0:T(8,128)(2,1)S(1)}) custom-call(bf16[8,768]{1,0:T(8,128)(2,1)S(1)} %copy-done.2, bf16[256,768]{1,0:T(8,128)(2,1)S(1)} %copy-done, bf16[256,768]{1,0:T(8,128)(2,1)S(1)} %copy-done.1, bf16[8,768]{1,0:T(8,128)(2,1)S(1)} %copy-done.3, ...), custom_call_target="tpu_custom_call" | custom-call | tf_op jit(solution)/shard_map/cross_attention_backward/pallas_call | solution.py:215
  24.5 0.6 %copy.13 = bf16[8,768]{1,0:T(8,128)(2,1)} copy(bf16[8,768]{1,0:T(8,128)(2,1)S(1)} %get-tuple-element.6) | data formatting | bytes 24576
  25.1 0.7 %copy.14 = bf16[256,768]{1,0:T(8,128)(2,1)} copy(bf16[256,768]{1,0:T(8,128)(2,1)S(1)} %get-tuple-element.7) | data formatting | bytes 786432
  25.9 0.7 %copy.15 = bf16[256,768]{1,0:T(8,128)(2,1)} copy(bf16[256,768]{1,0:T(8,128)(2,1)S(1)} %get-tuple-element.8) | data formatting | bytes 786432
Async XLA Ops:
  0.6 0.7 %copy-start.6 = (s32[8]{0:T(128)S(1)}, s32[8]{0:T(128)}, u32[]{:S(2)}) copy-start(s32[8]{0:T(128)} %param.13) | copy-start | bytes 100
  1.3 1.0 %copy-start = (bf16[256,768]{1,0:T(8,128)(2,1)S(1)}, bf16[256,768]{1,0:T(8,128)(2,1)}, u32[]{:S(2)}) copy-start(bf16[256,768]{1,0:T(8,128)(2,1)} %keys.1) | copy-start | bytes 1179652
  2.3 1.0 %copy-start.1 = (bf16[256,768]{1,0:T(8,128)(2,1)S(1)}, bf16[256,768]{1,0:T(8,128)(2,1)}, u32[]{:S(2)}) copy-start(bf16[256,768]{1,0:T(8,128)(2,1)} %values.1) | copy-start | bytes 1179652
  3.3 0.7 %copy-start.2 = (bf16[8,768]{1,0:T(8,128)(2,1)S(1)}, bf16[8,768]{1,0:T(8,128)(2,1)}, u32[]{:S(2)}) copy-start(bf16[8,768]{1,0:T(8,128)(2,1)} %query.1) | copy-start | bytes 36868
  4.0 0.7 %copy-start.3 = (bf16[8,768]{1,0:T(8,128)(2,1)S(1)}, bf16[8,768]{1,0:T(8,128)(2,1)}, u32[]{:S(2)}) copy-start(bf16[8,768]{1,0:T(8,128)(2,1)} %attn_out.1) | copy-start | bytes 36868
  4.7 0.7 %copy-start.4 = (bf16[8,768]{1,0:T(8,128)(2,1)S(1)}, bf16[8,768]{1,0:T(8,128)(2,1)}, u32[]{:S(2)}) copy-start(bf16[8,768]{1,0:T(8,128)(2,1)} %out_grad.1) | copy-start | bytes 36868
  5.4 0.7 %copy-start.5 = (f32[6,8]{1,0:T(8,128)S(1)}, f32[6,8]{1,0:T(8,128)}, u32[]{:S(2)}) copy-start(f32[6,8]{1,0:T(8,128)} %lse.1) | copy-start | bytes 580

commit v2 on v1

--- a/solution.py
+++ b/solution.py
@@ -26,11 +26,11 @@
 def kernel(
     n, heads, width,
     query, keys, values, attn_out, out_grad, lse, lengths,
-    dq_out, dk_out, dv_out,
+    dq, dk, dv,
     q_own, o_own, g_own, lse_own, len_own, k_in, v_in,
     msg, aux, msg_recv, aux_recv, q_all, g_all, p_all, s_all,
-    part, part_recv, own_part, dq, dk, dv,
-    in_sem, out_sem, aux_send, aux_sem, msg_send, msg_sem, part_send, part_sem,
+    part, part_recv, own_part,
+    in_sem, aux_send, aux_sem, msg_send, msg_sem, part_send, part_sem,
 ):
     me = lax.axis_index("blk")
     rows = q_own.shape[0]
@@ -162,7 +162,6 @@
         over(n - 1, send_part)
 
     tn = (((0,), (0,)), ((), ()))
-    results = []
     for g in range(groups):
         for j in range(HEADS_PER_GROUP):
             h = g * HEADS_PER_GROUP + j
@@ -170,10 +169,6 @@
             mine = slice(j * width, (j + 1) * width)
             dv[:, cols] = lax.dot_general(p_all[h], g_all[g, :, mine], tn, preferred_element_type=F32).astype(BF16)
             dk[:, cols] = lax.dot_general(s_all[h], q_all[g, :, mine], tn, preferred_element_type=F32).astype(BF16)
-    for i, (a, b) in enumerate([(dk, dk_out), (dv, dv_out)]):
-        copy = pltpu.make_async_copy(a, b, out_sem.at[i])
-        copy.start()
-        results.append(copy)
 
     for g in range(groups):
         all_of(part_recv.at[g], part_sem.at[g])
@@ -190,15 +185,21 @@
         for j in range(HEADS_PER_GROUP):
             h = g * HEADS_PER_GROUP + j
             dq[:, h * width : (h + 1) * width] = total[j * rows : (j + 1) * rows].astype(BF16)
-    copy = pltpu.make_async_copy(dq, dq_out, out_sem.at[2])
-    copy.start()
-    results.append(copy)
 
     all_of(aux_recv, aux_send)
     for g in range(groups):
         all_of(msg_recv.at[g], msg_send.at[g])
         all_of(part_recv.at[g], part_send.at[g])
-    for copy in results:
+
+
+def store(dq, dk, dv, dq_out, dk_out, dv_out, sem):
+    copies = [
+        pltpu.make_async_copy(a, b, sem.at[i])
+        for i, (a, b) in enumerate([(dk, dk_out), (dv, dv_out), (dq, dq_out)])
+    ]
+    for copy in copies:
+        copy.start()
+    for copy in copies:
         copy.wait()
 
 
@@ -209,10 +210,11 @@
     groups = heads // HEADS_PER_GROUP
     group_width = HEADS_PER_GROUP * width
     total = n * rows
-    anywhere = pl.BlockSpec(memory_space=pltpu.HBM)
+    anywhere = pl.BlockSpec(memory_space=pl.ANY)
     vmem = pltpu.VMEM
     dma = pltpu.SemaphoreType.DMA
-    return pl.pallas_call(
+    arrays = (query, keys, values, attn_out, out_grad, lse, lengths.reshape(1, rows))
+    grads = pl.pallas_call(
         functools.partial(kernel, n, heads, width),
         out_shape=(
             jax.ShapeDtypeStruct(query.shape, BF16),
@@ -220,7 +222,7 @@
             jax.ShapeDtypeStruct(values.shape, BF16),
         ),
         in_specs=[anywhere] * 7,
-        out_specs=(anywhere,) * 3,
+        out_specs=(pl.BlockSpec(memory_space=vmem),) * 3,
         scratch_shapes=[
             vmem(query.shape, BF16),
             vmem(query.shape, BF16),
@@ -240,11 +242,7 @@
             vmem((groups, n, HEADS_PER_GROUP * rows, width), BF16),
             vmem((groups, n, HEADS_PER_GROUP * rows, width), BF16),
             vmem((groups, HEADS_PER_GROUP * rows, width), F32),
-            vmem(query.shape, BF16),
-            vmem(keys.shape, BF16),
-            vmem(values.shape, BF16),
             dma((7,)),
-            dma((3,)),
             dma(()),
             dma(()),
             dma((groups,)),
@@ -256,7 +254,16 @@
             collective_id=0, has_side_effects=True, vmem_limit_bytes=40 * 1024 * 1024
         ),
         name="cross_attention_backward",
-    )(query, keys, values, attn_out, out_grad, lse, lengths.reshape(1, rows))
+    )(*[pltpu.with_memory_space_constraint(a, pltpu.HBM) for a in arrays])
+    return pl.pallas_call(
+        store,
+        out_shape=tuple(jax.ShapeDtypeStruct(a.shape, a.dtype) for a in grads),
+        in_specs=[pl.BlockSpec(memory_space=vmem)] * 3,
+        out_specs=(anywhere,) * 3,
+        scratch_shapes=[dma((3,))],
+        compiler_params=pltpu.CompilerParams(vmem_limit_bytes=4 * 1024 * 1024),
+        name="store_gradients",
+    )(*grads)
 
 
 def solution(mesh):

time: 27 us -> 19.8 us (0.73)
  local copies, waits for them, and re-layouts: 7.54 us -> 0 us
  Pallas kernels: 18.4 us -> 18.9 us
    unnamed x17 -> x0, local copies, waits for them, and re-layouts: 7.54 us -> none
    pallas_call x0 -> x1, Pallas kernels: none -> 0.91 us  [local(): pl.pallas_call(store, out_shape=tuple((jax.ShapeDtypeStruct(a.shape, a.dt...]
    pallas_call x1, Pallas kernels: 18.4 us -> 18 us  [local(): pl.pallas_call(functools.partial(kernel, n, heads, width), out_shape=(jax...]
where the time goes in v2:
time: 19.8 us; the launch traced here: 19.6 us
  Pallas kernels  18.9 us (95%)
  between operations  0.64 us (3%)
    pallas_call x1, Pallas kernels, local(): pl.pallas_call(functools.partial(kernel, n, heads, width), out_shape=(jax...  18 us
    pallas_call x1, Pallas kernels, local(): pl.pallas_call(store, out_shape=tuple((jax.ShapeDtypeStruct(a.shape, a.dt...  0.91 us

profile of v2, /device:TPU:0, one launch (start us, length us, event | category | flops | bytes accessed | tf_op | source)
XLA Modules:
  0.0 19.6 jit_solution(7544493542421466639)
XLA Ops:
  0.6 18.0 %cross_attention_backward.1 = (bf16[8,768]{1,0:T(8,128)(2,1)S(1)}, bf16[256,768]{1,0:T(8,128)(2,1)S(1)}, bf16[256,768]{1,0:T(8,128)(2,1)S(1)}) custom-call(bf16[8,768]{1,0:T(8,128)(2,1)} %query.1, bf16[256,768]{1,0:T(8,128)(2,1)} %keys.1, bf16[256,768]{1,0:T(8,128)(2,1)} %values.1, bf16[8,768]{1,0:T(8,128)(2,1)} %attn_out.1, bf16[8,768]{1,0:T(8,128)(2,1)} %out_grad.1, ...), custom_call_target="tpu_custom_call" | custom-call | tf_op jit(solution)/shard_map/cross_attention_backward/pallas_call | solution.py:217
  18.7 0.9 %store_gradients.1 = (bf16[8,768]{1,0:T(8,128)(2,1)}, bf16[256,768]{1,0:T(8,128)(2,1)}, bf16[256,768]{1,0:T(8,128)(2,1)}) custom-call(bf16[8,768]{1,0:T(8,128)(2,1)S(1)} %get-tuple-element.6.dq, bf16[256,768]{1,0:T(8,128)(2,1)S(1)} %get-tuple-element.7.dk, bf16[256,768]{1,0:T(8,128)(2,1)S(1)} %get-tuple-element.8.dv), custom_call_target="tpu_custom_call" | custom-call | tf_op jit(solution)/shard_map/store_gradients/pallas_call | solution.py:258

commit v3 on v2

--- a/solution.py
+++ b/solution.py
@@ -10,17 +10,18 @@
 
 HEADS_PER_GROUP = 2
 CHUNK_SLOTS = 8
+SEND_ORDER = (0, 1)
 UNROLL_LIMIT = 16
 F32 = jnp.float32
 BF16 = jnp.bfloat16
 
 
-def over(count, body):
-    if count <= UNROLL_LIMIT:
-        for i in range(count):
+def over(low, high, body):
+    if high - low <= UNROLL_LIMIT:
+        for i in reversed(range(low, high)):
             body(i)
     else:
-        lax.fori_loop(0, count, lambda i, c: (body(i), c)[1], 0)
+        lax.fori_loop(low, high, lambda i, c: (body(high - 1 + low - i), c)[1], 0)
 
 
 def kernel(
@@ -38,8 +39,18 @@
     group_width = HEADS_PER_GROUP * width
     groups = heads // HEADS_PER_GROUP
     scale = 1.0 / math.sqrt(width)
-    chunk_slots = min(n, CHUNK_SLOTS)
+    chunk_slots = min(n // 2, CHUNK_SLOTS)
     chunk_rows = chunk_slots * rows
+    classes = [(0, n // 2), (n // 2, n)]
+
+    barrier = pltpu.get_barrier_semaphore()
+
+    def greet(i):
+        pl.semaphore_signal(
+            barrier, inc=1, device_id={"blk": jnp.bitwise_xor(me, i)}, device_id_type=pl.DeviceIdType.MESH
+        )
+
+    over(1, n, greet)
 
     small = [(query, q_own), (attn_out, o_own), (out_grad, g_own), (lse, lse_own), (lengths, len_own)]
     large = [(keys, k_in), (values, v_in)]
@@ -47,15 +58,6 @@
     for copy in copies:
         copy.start()
 
-    barrier = pltpu.get_barrier_semaphore()
-
-    def greet(i):
-        pl.semaphore_signal(
-            barrier, inc=1, device_id={"blk": lax.rem(me + i + 1, n)}, device_id_type=pl.DeviceIdType.MESH
-        )
-
-    over(n - 1, greet)
-
     for copy in copies[: len(small)]:
         copy.wait()
     q32, g32 = q_own[...].astype(F32), g_own[...].astype(F32)
@@ -63,7 +65,7 @@
     for g in range(groups):
         piece = own[:, g * group_width : (g + 1) * group_width]
         msg[g] = piece
-        msg_recv[g, n - 1] = piece
+        msg_recv[g, 0] = piece
     product = g32 * o_own[...].astype(F32)
     lane = lax.broadcasted_iota(jnp.int32, (rows, 128), 1)
     eye = lax.broadcasted_iota(jnp.int32, (rows, rows), 0) == lax.broadcasted_iota(jnp.int32, (rows, rows), 1)
@@ -77,7 +79,7 @@
         table = jnp.where(lane == h, column(lse_own[h : h + 1, :]), table)
         table = jnp.where(lane == heads + h, delta, table)
     aux[...] = table
-    aux_recv[n - 1] = table
+    aux_recv[0] = table
 
     pl.semaphore_wait(barrier, n - 1)
 
@@ -88,20 +90,23 @@
         )
 
     def send_aux(i):
-        remote(aux, aux_recv.at[i], aux_send, aux_sem, lax.rem(me + i + 1, n)).start()
-
-    over(n - 1, send_aux)
-    for g in range(groups):
-
-        def send_msg(i, g=g):
-            remote(
-                msg.at[g], msg_recv.at[g, i], msg_send.at[g], msg_sem.at[g], lax.rem(me + i + 1, n)
-            ).start()
-
-        over(n - 1, send_msg)
-
-    def all_of(ref, sem):
-        whole = ref.at[pl.ds(0, n - 1)]
+        remote(aux, aux_recv.at[i], aux_send, aux_sem, jnp.bitwise_xor(me, i)).start()
+
+    over(1, n, send_aux)
+    for t in SEND_ORDER:
+        low, high = classes[t]
+        for g in range(groups):
+
+            def send_msg(i, g=g, t=t):
+                remote(
+                    msg.at[g], msg_recv.at[g, i], msg_send.at[g, t], msg_sem.at[g, t], jnp.bitwise_xor(me, i)
+                ).start()
+
+            over(max(low, 1), high, send_msg)
+
+    def all_of(ref, sem, low=1, high=n):
+        low = max(low, 1)
+        whole = ref.at[pl.ds(low, high - low)]
         pltpu.make_async_copy(whole, whole, sem).wait()
 
     for copy in copies[len(small) :]:
@@ -111,55 +116,56 @@
     position = me * key_rows + lax.broadcasted_iota(jnp.int32, (chunk_rows, key_rows), 1)
     position = position.astype(F32)
 
-    for g in range(groups):
-        all_of(msg_recv.at[g], msg_sem.at[g])
-
-        def attend(c, g=g):
-            slots = pl.ds(c * chunk_slots, chunk_slots)
-            lines = pl.ds(c * chunk_rows, chunk_rows)
-            got = msg_recv[g, slots].astype(F32)
-            q_c = got[:, :rows].reshape(chunk_rows, group_width).astype(BF16)
-            g_c = got[:, rows:].reshape(chunk_rows, group_width).astype(BF16)
-            q_all[g, lines] = q_c
-            g_all[g, lines] = g_c
-            facts = aux_recv[slots].reshape(chunk_rows, 128)
-            visible = position < facts[:, 2 * heads : 2 * heads + 1]
-            parts = []
-            for j in range(HEADS_PER_GROUP):
-                h = g * HEADS_PER_GROUP + j
-                cols = slice(h * width, (h + 1) * width)
-                mine = slice(j * width, (j + 1) * width)
-                k_h, v_h = k_in[:, cols], v_in[:, cols]
-                nt = (((1,), (1,)), ((), ()))
-                scores = lax.dot_general(q_c[:, mine], k_h, nt, preferred_element_type=F32) * scale
-                probs = jnp.where(visible, jnp.exp(scores - facts[:, h : h + 1]), 0.0)
-                prob_grad = lax.dot_general(g_c[:, mine], v_h, nt, preferred_element_type=F32)
-                delta = facts[:, heads + h : heads + h + 1]
-                score_grad = (probs * (prob_grad - delta) * scale).astype(BF16)
-                p_all[h, lines] = probs.astype(BF16)
-                s_all[h, lines] = score_grad
-                term = jnp.dot(score_grad, k_h, preferred_element_type=F32)
-                parts.append(term.reshape(chunk_slots, rows, width))
-            terms = jnp.concatenate(parts, axis=1)
-            part[g, slots] = terms.astype(BF16)
-            return terms
-
-        if n == chunk_slots:
-            own_part[g] = attend(0)[n - 1]
-        else:
-
-            def step(c, carry):
-                own_part[g] = attend(c)[chunk_slots - 1]
-                return carry
-
-            lax.fori_loop(0, n // chunk_slots, step, 0)
-
-        def send_part(i, g=g):
-            remote(
-                part.at[g, i], part_recv.at[g, i], part_send.at[g], part_sem.at[g], lax.rem(me + n - i - 1, n)
-            ).start()
-
-        over(n - 1, send_part)
+    for t, (low, high) in enumerate(classes):
+        for g in range(groups):
+            all_of(msg_recv.at[g], msg_sem.at[g, t], low, high)
+
+            def attend(c, g=g):
+                slots = pl.ds(c * chunk_slots, chunk_slots)
+                lines = pl.ds(c * chunk_rows, chunk_rows)
+                got = msg_recv[g, slots].astype(F32)
+                q_c = got[:, :rows].reshape(chunk_rows, group_width).astype(BF16)
+                g_c = got[:, rows:].reshape(chunk_rows, group_width).astype(BF16)
+                q_all[g, lines] = q_c
+                g_all[g, lines] = g_c
+                facts = aux_recv[slots].reshape(chunk_rows, 128)
+                visible = position < facts[:, 2 * heads : 2 * heads + 1]
+                parts = []
+                for j in range(HEADS_PER_GROUP):
+                    h = g * HEADS_PER_GROUP + j
+                    cols = slice(h * width, (h + 1) * width)
+                    mine = slice(j * width, (j + 1) * width)
+                    k_h, v_h = k_in[:, cols], v_in[:, cols]
+                    nt = (((1,), (1,)), ((), ()))
+                    scores = lax.dot_general(q_c[:, mine], k_h, nt, preferred_element_type=F32) * scale
+                    probs = jnp.where(visible, jnp.exp(scores - facts[:, h : h + 1]), 0.0)
+                    prob_grad = lax.dot_general(g_c[:, mine], v_h, nt, preferred_element_type=F32)
+                    delta = facts[:, heads + h : heads + h + 1]
+                    score_grad = (probs * (prob_grad - delta) * scale).astype(BF16)
+                    p_all[h, lines] = probs.astype(BF16)
+                    s_all[h, lines] = score_grad
+                    term = jnp.dot(score_grad, k_h, preferred_element_type=F32)
+                    parts.append(term.reshape(chunk_slots, rows, width))
+                terms = jnp.concatenate(parts, axis=1)
+                part[g, slots] = terms.astype(BF16)
+                return terms
+
+            first, last = low // chunk_slots, high // chunk_slots
+            if last - first == 1:
+                terms = attend(first)
+                if t == 0:
+                    own_part[g] = terms[0]
+            else:
+                if t == 0:
+                    own_part[g] = attend(0)[0]
+                lax.fori_loop(max(first, 1), last, lambda c, carry, attend=attend: (attend(c), carry)[1], 0)
+
+            def send_part(i, g=g, t=t):
+                remote(
+                    part.at[g, i], part_recv.at[g, i], part_send.at[g, t], part_sem.at[g, t], jnp.bitwise_xor(me, i)
+                ).start()
+
+            over(max(low, 1), high, send_part)
 
     tn = (((0,), (0,)), ((), ()))
     for g in range(groups):
@@ -171,25 +177,27 @@
             dk[:, cols] = lax.dot_general(s_all[h], q_all[g, :, mine], tn, preferred_element_type=F32).astype(BF16)
 
     for g in range(groups):
-        all_of(part_recv.at[g], part_sem.at[g])
+        for t, (low, high) in enumerate(classes):
+            all_of(part_recv.at[g], part_sem.at[g, t], low, high)
 
         def add(i, total, g=g):
             return total + part_recv[g, i].astype(F32)
 
         total = own_part[g]
         if n <= UNROLL_LIMIT:
-            for i in range(n - 1):
+            for i in range(1, n):
                 total = add(i, total)
         else:
-            total = lax.fori_loop(0, n - 1, add, total)
+            total = lax.fori_loop(1, n, add, total)
         for j in range(HEADS_PER_GROUP):
             h = g * HEADS_PER_GROUP + j
             dq[:, h * width : (h + 1) * width] = total[j * rows : (j + 1) * rows].astype(BF16)
 
     all_of(aux_recv, aux_send)
     for g in range(groups):
-        all_of(msg_recv.at[g], msg_send.at[g])
-        all_of(part_recv.at[g], part_send.at[g])
+        for t, (low, high) in enumerate(classes):
+            all_of(msg_recv.at[g], msg_send.at[g, t], low, high)
+            all_of(part_recv.at[g], part_send.at[g, t], low, high)
 
 
 def store(dq, dk, dv, dq_out, dk_out, dv_out, sem):
@@ -245,10 +253,10 @@
             dma((7,)),
             dma(()),
             dma(()),
-            dma((groups,)),
-            dma((groups,)),
-            dma((groups,)),
-            dma((groups,)),
+            dma((groups, 2)),
+            dma((groups, 2)),
+            dma((groups, 2)),
+            dma((groups, 2)),
         ],
         compiler_params=pltpu.CompilerParams(
             collective_id=0, has_side_effects=True, vmem_limit_bytes=40 * 1024 * 1024

time: 19.8 us -> 19 us (0.960)
  Pallas kernels: 18.9 us -> 18.2 us
    pallas_call x1, Pallas kernels: 18 us -> 17.2 us  [local(): pl.pallas_call(functools.partial(kernel, n, heads, width), out_shape=(jax...]
where the time goes in v3:
time: 19 us; the launch traced here: 18.8 us
  Pallas kernels  18.2 us (96%)
  between operations  0.64 us (3%)
    pallas_call x1, Pallas kernels, local(): pl.pallas_call(functools.partial(kernel, n, heads, width), out_shape=(jax...  17.2 us
    pallas_call x1, Pallas kernels, local(): pl.pallas_call(store, out_shape=tuple((jax.ShapeDtypeStruct(a.shape, a.dt...  0.91 us

profile of v3, /device:TPU:0, one launch (start us, length us, event | category | flops | bytes accessed | tf_op | source)
XLA Modules:
  0.0 18.8 jit_solution(4916453584171485979)
XLA Ops:
  0.6 17.2 %cross_attention_backward.1 = (bf16[8,768]{1,0:T(8,128)(2,1)S(1)}, bf16[256,768]{1,0:T(8,128)(2,1)S(1)}, bf16[256,768]{1,0:T(8,128)(2,1)S(1)}) custom-call(bf16[8,768]{1,0:T(8,128)(2,1)} %query.1, bf16[256,768]{1,0:T(8,128)(2,1)} %keys.1, bf16[256,768]{1,0:T(8,128)(2,1)} %values.1, bf16[8,768]{1,0:T(8,128)(2,1)} %attn_out.1, bf16[8,768]{1,0:T(8,128)(2,1)} %out_grad.1, ...), custom_call_target="tpu_custom_call" | custom-call | tf_op jit(solution)/shard_map/cross_attention_backward/pallas_call | solution.py:225
  17.9 0.9 %store_gradients.1 = (bf16[8,768]{1,0:T(8,128)(2,1)}, bf16[256,768]{1,0:T(8,128)(2,1)}, bf16[256,768]{1,0:T(8,128)(2,1)}) custom-call(bf16[8,768]{1,0:T(8,128)(2,1)S(1)} %get-tuple-element.6.dq, bf16[256,768]{1,0:T(8,128)(2,1)S(1)} %get-tuple-element.7.dk, bf16[256,768]{1,0:T(8,128)(2,1)S(1)} %get-tuple-element.8.dv), custom_call_target="tpu_custom_call" | custom-call | tf_op jit(solution)/shard_map/store_gradients/pallas_call | solution.py:266

commit v4 on v3

--- a/solution.py
+++ b/solution.py
@@ -29,7 +29,7 @@
     query, keys, values, attn_out, out_grad, lse, lengths,
     dq, dk, dv,
     q_own, o_own, g_own, lse_own, len_own, k_in, v_in,
-    msg, aux, msg_recv, aux_recv, q_all, g_all, p_all, s_all,
+    msg, aux, msg_recv, aux_recv, q_all, g_all, p_all, s_all, k_turned, v_turned,
     part, part_recv, own_part,
     in_sem, aux_send, aux_sem, msg_send, msg_sem, part_send, part_sem,
 ):
@@ -89,12 +89,12 @@
             device_id={"blk": peer}, device_id_type=pl.DeviceIdType.MESH,
         )
 
-    def send_aux(i):
-        remote(aux, aux_recv.at[i], aux_send, aux_sem, jnp.bitwise_xor(me, i)).start()
-
-    over(1, n, send_aux)
+    def send_aux(i, t):
+        remote(aux, aux_recv.at[i], aux_send.at[t], aux_sem.at[t], jnp.bitwise_xor(me, i)).start()
+
     for t in SEND_ORDER:
         low, high = classes[t]
+        over(max(low, 1), high, functools.partial(send_aux, t=t))
         for g in range(groups):
 
             def send_msg(i, g=g, t=t):
@@ -111,12 +111,17 @@
 
     for copy in copies[len(small) :]:
         copy.wait()
-    all_of(aux_recv, aux_sem)
+
+    for h in range(heads):
+        cols = slice(h * width, (h + 1) * width)
+        k_turned[h] = k_in[:, cols].T
+        v_turned[h] = v_in[:, cols].T
 
     position = me * key_rows + lax.broadcasted_iota(jnp.int32, (chunk_rows, key_rows), 1)
     position = position.astype(F32)
 
     for t, (low, high) in enumerate(classes):
+        all_of(aux_recv, aux_sem.at[t], low, high)
         for g in range(groups):
             all_of(msg_recv.at[g], msg_sem.at[g, t], low, high)
 
@@ -135,11 +140,10 @@
                     h = g * HEADS_PER_GROUP + j
                     cols = slice(h * width, (h + 1) * width)
                     mine = slice(j * width, (j + 1) * width)
-                    k_h, v_h = k_in[:, cols], v_in[:, cols]
-                    nt = (((1,), (1,)), ((), ()))
-                    scores = lax.dot_general(q_c[:, mine], k_h, nt, preferred_element_type=F32) * scale
+                    k_h = k_in[:, cols]
+                    scores = jnp.dot(q_c[:, mine], k_turned[h], preferred_element_type=F32) * scale
                     probs = jnp.where(visible, jnp.exp(scores - facts[:, h : h + 1]), 0.0)
-                    prob_grad = lax.dot_general(g_c[:, mine], v_h, nt, preferred_element_type=F32)
+                    prob_grad = jnp.dot(g_c[:, mine], v_turned[h], preferred_element_type=F32)
                     delta = facts[:, heads + h : heads + h + 1]
                     score_grad = (probs * (prob_grad - delta) * scale).astype(BF16)
                     p_all[h, lines] = probs.astype(BF16)
@@ -193,7 +197,8 @@
             h = g * HEADS_PER_GROUP + j
             dq[:, h * width : (h + 1) * width] = total[j * rows : (j + 1) * rows].astype(BF16)
 
-    all_of(aux_recv, aux_send)
+    for t, (low, high) in enumerate(classes):
+        all_of(aux_recv, aux_send.at[t], low, high)
     for g in range(groups):
         for t, (low, high) in enumerate(classes):
             all_of(msg_recv.at[g], msg_send.at[g, t], low, high)
@@ -247,12 +252,14 @@
             vmem((groups, total, group_width), BF16),
             vmem((heads, total, key_rows), BF16),
             vmem((heads, total, key_rows), BF16),
+            vmem((heads, width, key_rows), BF16),
+            vmem((heads, width, key_rows), BF16),
             vmem((groups, n, HEADS_PER_GROUP * rows, width), BF16),
             vmem((groups, n, HEADS_PER_GROUP * rows, width), BF16),
             vmem((groups, HEADS_PER_GROUP * rows, width), F32),
             dma((7,)),
-            dma(()),
-            dma(()),
+            dma((2,)),
+            dma((2,)),
             dma((groups, 2)),
             dma((groups, 2)),
             dma((groups, 2)),

time: 19 us -> 19 us (level)
  no operation moved by 1% of the time
where the time goes in v4:
time: 19 us; the launch traced here: 18.8 us
  Pallas kernels  18.2 us (96%)
  between operations  0.64 us (3%)
    pallas_call x1, Pallas kernels, local(): pl.pallas_call(functools.partial(kernel, n, heads, width), out_shape=(jax...  17.3 us
    pallas_call x1, Pallas kernels, local(): pl.pallas_call(store, out_shape=tuple((jax.ShapeDtypeStruct(a.shape, a.dt...  0.91 us

profile of v4, /device:TPU:0, one launch (start us, length us, event | category | flops | bytes accessed | tf_op | source)
XLA Modules:
  0.0 18.8 jit_solution(8594890483541922862)
XLA Ops:
  0.6 17.3 %cross_attention_backward.1 = (bf16[8,768]{1,0:T(8,128)(2,1)S(1)}, bf16[256,768]{1,0:T(8,128)(2,1)S(1)}, bf16[256,768]{1,0:T(8,128)(2,1)S(1)}) custom-call(bf16[8,768]{1,0:T(8,128)(2,1)} %query.1, bf16[256,768]{1,0:T(8,128)(2,1)} %keys.1, bf16[256,768]{1,0:T(8,128)(2,1)} %values.1, bf16[8,768]{1,0:T(8,128)(2,1)} %attn_out.1, bf16[8,768]{1,0:T(8,128)(2,1)} %out_grad.1, ...), custom_call_target="tpu_custom_call" | custom-call | tf_op jit(solution)/shard_map/cross_attention_backward/pallas_call | solution.py:230
  17.9 0.9 %store_gradients.1 = (bf16[8,768]{1,0:T(8,128)(2,1)}, bf16[256,768]{1,0:T(8,128)(2,1)}, bf16[256,768]{1,0:T(8,128)(2,1)}) custom-call(bf16[8,768]{1,0:T(8,128)(2,1)S(1)} %get-tuple-element.6.dq, bf16[256,768]{1,0:T(8,128)(2,1)S(1)} %get-tuple-element.7.dk, bf16[256,768]{1,0:T(8,128)(2,1)S(1)} %get-tuple-element.8.dv), custom_call_target="tpu_custom_call" | custom-call | tf_op jit(solution)/shard_map/store_gradients/pallas_call | solution.py:273

commit v5 on v4

--- a/solution.py
+++ b/solution.py
@@ -112,10 +112,10 @@
     for copy in copies[len(small) :]:
         copy.wait()
 
-    for h in range(heads):
-        cols = slice(h * width, (h + 1) * width)
-        k_turned[h] = k_in[:, cols].T
-        v_turned[h] = v_in[:, cols].T
+    for g in range(groups):
+        cols = slice(g * group_width, (g + 1) * group_width)
+        k_turned[g] = k_in[:, cols].T
+        v_turned[g] = v_in[:, cols].T
 
     position = me * key_rows + lax.broadcasted_iota(jnp.int32, (chunk_rows, key_rows), 1)
     position = position.astype(F32)
@@ -136,19 +136,29 @@
                 facts = aux_recv[slots].reshape(chunk_rows, 128)
                 visible = position < facts[:, 2 * heads : 2 * heads + 1]
                 parts = []
-                for j in range(HEADS_PER_GROUP):
-                    h = g * HEADS_PER_GROUP + j
-                    cols = slice(h * width, (h + 1) * width)
-                    mine = slice(j * width, (j + 1) * width)
-                    k_h = k_in[:, cols]
-                    scores = jnp.dot(q_c[:, mine], k_turned[h], preferred_element_type=F32) * scale
-                    probs = jnp.where(visible, jnp.exp(scores - facts[:, h : h + 1]), 0.0)
-                    prob_grad = jnp.dot(g_c[:, mine], v_turned[h], preferred_element_type=F32)
+                group = slice(g * group_width, (g + 1) * group_width)
+                heads_in = [g * HEADS_PER_GROUP + j for j in range(HEADS_PER_GROUP)]
+                head_of = lax.broadcasted_iota(jnp.int32, (chunk_rows, group_width), 1) // width
+
+                def spread(x):
+                    return jnp.concatenate(
+                        [jnp.where(head_of == j, x, jnp.zeros_like(x)) for j in range(HEADS_PER_GROUP)], axis=0
+                    )
+
+                scores = jnp.dot(spread(q_c), k_turned[g], preferred_element_type=F32) * scale
+                prob_grad = jnp.dot(spread(g_c), v_turned[g], preferred_element_type=F32)
+                grads = []
+                for j, h in enumerate(heads_in):
+                    block = slice(j * chunk_rows, (j + 1) * chunk_rows)
+                    probs = jnp.where(visible, jnp.exp(scores[block] - facts[:, h : h + 1]), 0.0)
                     delta = facts[:, heads + h : heads + h + 1]
-                    score_grad = (probs * (prob_grad - delta) * scale).astype(BF16)
+                    score_grad = (probs * (prob_grad[block] - delta) * scale).astype(BF16)
                     p_all[h, lines] = probs.astype(BF16)
                     s_all[h, lines] = score_grad
-                    term = jnp.dot(score_grad, k_h, preferred_element_type=F32)
+                    grads.append(score_grad)
+                both = jnp.dot(jnp.concatenate(grads, axis=0), k_in[:, group], preferred_element_type=F32)
+                for j in range(HEADS_PER_GROUP):
+                    term = both[j * chunk_rows : (j + 1) * chunk_rows, j * width : (j + 1) * width]
                     parts.append(term.reshape(chunk_slots, rows, width))
                 terms = jnp.concatenate(parts, axis=1)
                 part[g, slots] = terms.astype(BF16)
@@ -252,8 +262,8 @@
             vmem((groups, total, group_width), BF16),
             vmem((heads, total, key_rows), BF16),
             vmem((heads, total, key_rows), BF16),
-            vmem((heads, width, key_rows), BF16),
-            vmem((heads, width, key_rows), BF16),
+            vmem((groups, group_width, key_rows), BF16),
+            vmem((groups, group_width, key_rows), BF16),
             vmem((groups, n, HEADS_PER_GROUP * rows, width), BF16),
             vmem((groups, n, HEADS_PER_GROUP * rows, width), BF16),
             vmem((groups, HEADS_PER_GROUP * rows, width), F32),

time: 19 us -> 19.5 us (1.026)
  Pallas kernels: 18.2 us -> 18.6 us
    pallas_call x1, Pallas kernels: 17.3 us -> 17.7 us  [local(): pl.pallas_call(functools.partial(kernel, n, heads, width), out_shape=(jax...]
where the time goes in v5:
time: 19.5 us; the launch traced here: 19.3 us
  Pallas kernels  18.6 us (95%)
  between operations  0.64 us (3%)
    pallas_call x1, Pallas kernels, local(): pl.pallas_call(functools.partial(kernel, n, heads, width), out_shape=(jax...  17.7 us
    pallas_call x1, Pallas kernels, local(): pl.pallas_call(store, out_shape=tuple((jax.ShapeDtypeStruct(a.shape, a.dt...  0.91 us

profile of v5, /device:TPU:0, one launch (start us, length us, event | category | flops | bytes accessed | tf_op | source)
XLA Modules:
  0.0 19.3 jit_solution(3205627109678069570)
XLA Ops:
  0.6 17.7 %cross_attention_backward.1 = (bf16[8,768]{1,0:T(8,128)(2,1)S(1)}, bf16[256,768]{1,0:T(8,128)(2,1)S(1)}, bf16[256,768]{1,0:T(8,128)(2,1)S(1)}) custom-call(bf16[8,768]{1,0:T(8,128)(2,1)} %query.1, bf16[256,768]{1,0:T(8,128)(2,1)} %keys.1, bf16[256,768]{1,0:T(8,128)(2,1)} %values.1, bf16[8,768]{1,0:T(8,128)(2,1)} %attn_out.1, bf16[8,768]{1,0:T(8,128)(2,1)} %out_grad.1, ...), custom_call_target="tpu_custom_call" | custom-call | tf_op jit(solution)/shard_map/cross_attention_backward/pallas_call | solution.py:240
  18.4 0.9 %store_gradients.1 = (bf16[8,768]{1,0:T(8,128)(2,1)}, bf16[256,768]{1,0:T(8,128)(2,1)}, bf16[256,768]{1,0:T(8,128)(2,1)}) custom-call(bf16[8,768]{1,0:T(8,128)(2,1)S(1)} %get-tuple-element.6.dq, bf16[256,768]{1,0:T(8,128)(2,1)S(1)} %get-tuple-element.7.dk, bf16[256,768]{1,0:T(8,128)(2,1)S(1)} %get-tuple-element.8.dv), custom_call_target="tpu_custom_call" | custom-call | tf_op jit(solution)/shard_map/store_gradients/pallas_call | solution.py:283
